TPU v7x, 32 devices: a whole 2x2x4 slice. The times are simulated.
32 devices in a mesh: groups: 2 (over x), tensor: 4 (over y, core), section: 4 (over z).
Axes of the slice: x: 2, y: 2, z: 4, core: 2. Of those that a mesh axis runs over, the one named last changes fastest.
Arguments:
- prompt: bfloat16 [128, 8192], P(('groups', 'section'), 'tensor'), parts along dimension 0, may hold values from -6 to 6
- norm_gain: float32 [8, 8192], P(('groups', 'section')), parts along dimension 0, may hold values from 0.5 to 1.5
- kept_ranks: int32 [8, 3], P(('groups', 'section')), parts along dimension 0, may hold values from 128 to 512, as said below
- gate_left: bfloat16 [8, 512, 8192], P('groups', 'tensor', 'section'), parts along dimension 0, may hold values from -0.0625 to 0.0625
- up_left: bfloat16 [8, 512, 8192], P('groups', 'tensor', 'section'), parts along dimension 0, may hold values from -0.0625 to 0.0625
- gate_right: bfloat16 [8, 512, 14336], P('groups', 'tensor', 'section'), parts along dimension 0, may hold values from -0.375 to 0.375
- up_right: bfloat16 [8, 512, 14336], P('groups', 'tensor', 'section'), parts along dimension 0, may hold values from -0.375 to 0.375
- down_left: bfloat16 [8, 512, 14336], P('groups', 'tensor', 'section'), parts along dimension 0, may hold values from -0.046875 to 0.046875
- down_right: bfloat16 [8, 8192, 512], P('groups', 'tensor', 'section'), parts along dimension 0, may hold values from -0.5 to 0.5
Outputs:
- final_stream: bfloat16 [128, 8192], P(('groups', 'section'), 'tensor'), parts along dimension 0
There are 2 independent parts, one for each index of `groups`. A program takes and returns all parts, laid end to end along the dimension named above; each array names one. Nothing has to cross between parts.
Inputs may be any that keep to these rules, and one draw needn't show every extreme that they name: `kept_ranks`: column 0, 1, 2 holds the rank kept for the gate, up and down matrices; the value 512 occurs in every draw.
All inputs are finite; a program needn't handle non-finite values.
Results may differ from a plain program's by a relative error of at most 0.035.
Values may be sent and summed in bfloat16 or wider, within the bound.
A program may use at most 128 MiB of HBM per device.

v0:
```python
import jax
import jax.numpy as jnp
from jax import lax
from jax.sharding import PartitionSpec as P

RMAX = 512


def from_behind(block, axis, distance):
    devices = range(lax.axis_size(axis))
    route = [(i - distance, i) for i in devices if i - distance in devices]
    return lax.ppermute(block, axis, route)


def broadcast(array, axis, root):
    mine = lax.axis_index(axis) == root
    return lax.psum(jnp.where(mine, array, jnp.zeros_like(array)), axis)


def contract_last(left_side, right_side):
    return lax.dot_general(
        left_side, right_side, (((1,), (1,)), ((), ())), preferred_element_type=jnp.float32
    )


def body(
    prompt, norm_gain, kept_ranks, gate_left, up_left, gate_right, up_right, down_left, down_right
):
    section_count = lax.axis_size("section")
    tensor_rank = lax.axis_index("tensor")
    section_rank = lax.axis_index("section")
    gate_rows, up_rows, down_cols = (
        lax.all_to_all(gate_left, "section", split_axis=0, concat_axis=2, tiled=True),
        lax.all_to_all(up_left, "section", split_axis=0, concat_axis=2, tiled=True),
        lax.all_to_all(down_right, "section", split_axis=0, concat_axis=2, tiled=True),
    )
    gate_cols, up_cols, down_rows = (
        lax.all_to_all(
            lax.all_to_all(gate_right, "tensor", split_axis=2, concat_axis=1, tiled=True),
            "section",
            split_axis=0,
            concat_axis=2,
            tiled=True,
        ),
        lax.all_to_all(
            lax.all_to_all(up_right, "tensor", split_axis=2, concat_axis=1, tiled=True),
            "section",
            split_axis=0,
            concat_axis=2,
            tiled=True,
        ),
        lax.all_to_all(
            lax.all_to_all(down_left, "tensor", split_axis=2, concat_axis=1, tiled=True),
            "section",
            split_axis=0,
            concat_axis=2,
            tiled=True,
        ),
    )
    gate_rows, up_rows, down_cols = (gate_rows[0], up_rows[0], down_cols[0])
    gate_cols, up_cols, down_rows = (gate_cols[0], up_cols[0], down_rows[0])
    rank_block = gate_rows.shape[0]
    column_block = down_cols.shape[0]
    micro_rows = prompt.shape[0]
    positions = tensor_rank * rank_block + jnp.arange(rank_block, dtype=jnp.int32)
    gate_mask = (positions < kept_ranks[0, 0]).astype(jnp.float32)
    up_mask = (positions < kept_ranks[0, 1]).astype(jnp.float32)
    down_mask = (jnp.arange(RMAX, dtype=jnp.int32) < kept_ranks[0, 2]).astype(jnp.float32)
    norm_scale = norm_gain[0]
    own_start = tensor_rank * column_block
    prompt_rows = lax.all_gather(prompt, "section", axis=0, tiled=True)

    def layer_step(stream):
        float_stream = stream.astype(jnp.float32)
        variance = jnp.mean(float_stream * float_stream, axis=-1, keepdims=True)
        normed = (float_stream * lax.rsqrt(variance + 1e-05) * norm_scale).astype(jnp.bfloat16)
        gate_part = (contract_last(normed, gate_rows) * gate_mask).astype(jnp.bfloat16)
        up_part = (contract_last(normed, up_rows) * up_mask).astype(jnp.bfloat16)
        gate_low, up_low = (
            lax.all_gather(gate_part, "tensor", axis=1, tiled=True),
            lax.all_gather(up_part, "tensor", axis=1, tiled=True),
        )
        gate_values = jnp.dot(gate_low, gate_cols, preferred_element_type=jnp.float32)
        up_values = jnp.dot(up_low, up_cols, preferred_element_type=jnp.float32)
        hidden = (jax.nn.silu(gate_values) * up_values).astype(jnp.bfloat16)
        summed = lax.psum(contract_last(hidden, down_rows), "tensor")
        down_low = (summed * down_mask).astype(jnp.bfloat16)
        branch = contract_last(down_low, down_cols)
        own_columns = lax.dynamic_slice_in_dim(float_stream, own_start, column_block, 1)
        return (own_columns + branch).astype(jnp.bfloat16)

    incoming = jnp.zeros((micro_rows, column_block), jnp.bfloat16)
    results = jnp.zeros((micro_rows * section_count, column_block), jnp.bfloat16)

    def tick_body(tick_index, carry):
        incoming, results = carry
        entering = lax.dynamic_slice_in_dim(
            prompt_rows, jnp.minimum(tick_index, section_count - 1) * micro_rows, micro_rows, 0
        )
        current = jnp.where((section_rank == 0) & (tick_index < section_count), entering, incoming)
        stream = lax.all_gather(current, "tensor", axis=1, tiled=True)
        new_part = layer_step(stream)
        incoming = from_behind(new_part, "section", 1)
        finished = tick_index - (section_count - 1)
        slot_start = jnp.maximum(finished, 0) * micro_rows
        updated = lax.dynamic_update_slice_in_dim(results, new_part, slot_start, 0)
        results = jnp.where((section_rank == section_count - 1) & (finished >= 0), updated, results)
        return (incoming, results)

    incoming, results = lax.fori_loop(0, 2 * section_count - 1, tick_body, (incoming, results))
    delivered = broadcast(results, "section", section_count - 1)
    return lax.dynamic_slice_in_dim(delivered, section_rank * micro_rows, micro_rows, 0)


def solution(mesh):
    in_specs = (
        P(("groups", "section"), "tensor"),
        P(("groups", "section"), None),
        P(("groups", "section"), None),
        P("groups", "tensor", "section"),
        P("groups", "tensor", "section"),
        P("groups", "tensor", "section"),
        P("groups", "tensor", "section"),
        P("groups", "tensor", "section"),
        P("groups", "tensor", "section"),
    )
    out_specs = P(("groups", "section"), "tensor")
    return jax.shard_map(body, mesh=mesh, in_specs=in_specs, out_specs=out_specs, check_vma=False)
```

profile of v0, /device:TPU:0, one launch (start us, length us, event | category | flops | bytes accessed | tf_op | source)
XLA Modules:
  0.0 1002.8 jit_solution(816205238414276463)
XLA Ops:
  6.5 6.8 copy.26
  13.4 4.8 all-to-all-start.1
  18.2 6.9 copy.30
  25.0 36.3 %all-to-all-done.1 = bf16[4,128,3584]{1,0,2:T(4,128)(2,1)} async-done(((bf16[4,128,3584]{1,0,2:T(4,128)(2,1)}), bf16[4,128,3584]{1,0,2:T(4,128)(2,1)}, u32[]{:S(2)}, u32[]{:S(2)}) %all-to-all-start.1) | async-done | bytes 3670048 | tf_op jit(solution)/shard_map/all_to_all | solution.py:39
  61.4 4.7 all-to-all-start.4
  66.1 6.9 copy.33
  73.0 35.7 %all-to-all-done.4 = bf16[4,128,3584]{1,0,2:T(4,128)(2,1)} async-done(((bf16[4,128,3584]{1,0,2:T(4,128)(2,1)}), bf16[4,128,3584]{1,0,2:T(4,128)(2,1)}, u32[]{:S(2)}, u32[]{:S(2)}) %all-to-all-start.4) | async-done | bytes 3670048 | tf_op jit(solution)/shard_map/all_to_all | solution.py:46
  108.7 48.1 %all_to_all.144 = bf16[4,128,3584]{1,0,2:T(4,128)(2,1)} all-to-all(bf16[4,128,3584]{1,0,2:T(4,128)(2,1)} %copy.33), channel_id=1, replica_groups=mesh['groups'=2,'tensor'=4,'section'=4] {'tensor'}, dimensions={2} | all-to-all | bytes 7340032 | tf_op jit(solution)/shard_map/all_to_all | solution.py:53
  156.9 53.6 %all_to_all.145 = bf16[4,128,2048]{2,1,0:T(8,128)(2,1)} all-to-all(bf16[4,128,2048]{2,1,0:T(8,128)(2,1)S(1)} %copy-done.6), channel_id=1, replica_groups=mesh['groups'=2,'tensor'=4,'section'=4] {'section'}, dimensions={0} | all-to-all | bytes 4194304 | tf_op jit(solution)/shard_map/all_to_all | solution.py:33
  210.5 50.5 %all_to_all.146 = bf16[4,128,2048]{2,1,0:T(8,128)(2,1)} all-to-all(bf16[4,128,2048]{2,1,0:T(8,128)(2,1)S(1)} %copy-done.7), channel_id=1, replica_groups=mesh['groups'=2,'tensor'=4,'section'=4] {'section'}, dimensions={0} | all-to-all | bytes 4194304 | tf_op jit(solution)/shard_map/all_to_all | solution.py:34
  264.6 6.9 copy.27
  271.4 40.4 %all-to-all-done.8 = bf16[4,2048,128]{2,1,0:T(8,128)(2,1)S(1)} async-done(((bf16[4,2048,128]{2,1,0:T(8,128)(2,1)}), bf16[4,2048,128]{2,1,0:T(8,128)(2,1)S(1)}, u32[]{:S(2)}, u32[]{:S(2)}) %all-to-all-start.8) | async-done | bytes 2097184 | tf_op jit(solution)/shard_map/all_to_all | solution.py:35
  313.1 4.8 all-to-all-start.2
  317.9 6.9 copy.31
  324.8 74.6 %all-to-all-done.2 = bf16[4,512,896]{2,1,0:T(8,128)(2,1)} async-done(((bf16[4,512,896]{2,1,0:T(8,128)(2,1)}), bf16[4,512,896]{2,1,0:T(8,128)(2,1)}, u32[]{:S(2)}, u32[]{:S(2)}) %all-to-all-start.2) | async-done | bytes 3670048 | tf_op jit(solution)/shard_map/all_to_all | solution.py:38
  399.4 4.7 all-to-all-start.5
  404.1 7.0 copy.34
  411.1 74.5 %all-to-all-done.5 = bf16[4,512,896]{2,1,0:T(8,128)(2,1)} async-done(((bf16[4,512,896]{2,1,0:T(8,128)(2,1)}), bf16[4,512,896]{2,1,0:T(8,128)(2,1)}, u32[]{:S(2)}, u32[]{:S(2)}) %all-to-all-start.5) | async-done | bytes 3670048 | tf_op jit(solution)/shard_map/all_to_all | solution.py:45
  485.6 4.9 all-to-all-start.7
  490.6 89.0 %all_gather.33 = bf16[64,2048]{1,0:T(8,128)(2,1)S(1)} all-gather(bf16[16,2048]{1,0:T(8,128)(2,1)S(1)} %copy-done.8), channel_id=1, replica_groups=mesh['groups'=2,'tensor'=4,'section'=4] {'section'}, dimensions={0}, use_global_device_ids=true | all-gather | bytes 327680 | tf_op jit(solution)/shard_map/all_gather | solution.py:71
  587.6 9.7 copy.36
  599.1 6.0 copy.28
  605.1 5.9 copy.37
  611.0 6.0 copy.32
  616.9 6.0 copy.38
  622.9 6.0 copy.35
  628.9 6.0 copy.39
  634.9 321.8 %while.19 = (s32[]{:T(128)}, bf16[16,2048]{1,0:T(8,128)(2,1)S(1)}, bf16[64,2048]{1,0:T(8,128)(2,1)S(1)}, pred[]{:T(512)}, bf16[64,2048]{1,0:T(8,128)(2,1)S(1)}, ...) while((s32[]{:T(128)}, bf16[16,2048]{1,0:T(8,128)(2,1)S(1)}, ...), condition=%wide.region_3.4_spmd.clone.clone, body=%wide.region_0.3_spmd.clone.clone.sunk | while | flops 278906656 | bytes 35412760 | solution.py:110
  635.0 5.8 all_gather.43
  642.5 5.2 all_gather.45
  650.6 5.2 all_gather.44
  656.4 4.7 fusion.54
  661.1 11.0 %psum.25 = f32[16,512]{1,0:T(8,128)S(1)} all-reduce(f32[16,512]{1,0:T(8,128)S(1)} %fusion.54), channel_id=1, replica_groups=mesh['groups'=2,'tensor'=4,'section'=4] {'tensor'}, use_global_device_ids=true, to_apply=%region_2.2 | all-reduce | flops 8192 | bytes 65536 | tf_op jit(solution)/shard_map/while/body/eval_jaxpr/psum | solution.py:86
  679.7 5.8 all_gather.43
  687.2 5.2 all_gather.45
  695.3 5.2 all_gather.44
  701.1 4.7 fusion.54
  705.7 11.2 %psum.25 = f32[16,512]{1,0:T(8,128)S(1)} all-reduce(f32[16,512]{1,0:T(8,128)S(1)} %fusion.54), channel_id=1, replica_groups=mesh['groups'=2,'tensor'=4,'section'=4] {'tensor'}, use_global_device_ids=true, to_apply=%region_2.2 | all-reduce | flops 8192 | bytes 65536 | tf_op jit(solution)/shard_map/while/body/eval_jaxpr/psum | solution.py:86
  726.0 5.8 all_gather.43
  733.5 5.2 all_gather.45
  741.6 5.2 all_gather.44
  747.4 4.7 fusion.54
  752.0 11.0 %psum.25 = f32[16,512]{1,0:T(8,128)S(1)} all-reduce(f32[16,512]{1,0:T(8,128)S(1)} %fusion.54), channel_id=1, replica_groups=mesh['groups'=2,'tensor'=4,'section'=4] {'tensor'}, use_global_device_ids=true, to_apply=%region_2.2 | all-reduce | flops 8192 | bytes 65536 | tf_op jit(solution)/shard_map/while/body/eval_jaxpr/psum | solution.py:86
  772.0 5.8 all_gather.43
  779.6 5.2 all_gather.45
  787.6 5.2 all_gather.44
  793.4 4.7 fusion.54
  798.1 11.2 %psum.25 = f32[16,512]{1,0:T(8,128)S(1)} all-reduce(f32[16,512]{1,0:T(8,128)S(1)} %fusion.54), channel_id=1, replica_groups=mesh['groups'=2,'tensor'=4,'section'=4] {'tensor'}, use_global_device_ids=true, to_apply=%region_2.2 | all-reduce | flops 8192 | bytes 65536 | tf_op jit(solution)/shard_map/while/body/eval_jaxpr/psum | solution.py:86
  818.3 5.8 all_gather.43
  825.9 5.2 all_gather.45
  833.9 5.2 all_gather.44
  839.7 4.7 fusion.54
  844.4 11.0 %psum.25 = f32[16,512]{1,0:T(8,128)S(1)} all-reduce(f32[16,512]{1,0:T(8,128)S(1)} %fusion.54), channel_id=1, replica_groups=mesh['groups'=2,'tensor'=4,'section'=4] {'tensor'}, use_global_device_ids=true, to_apply=%region_2.2 | all-reduce | flops 8192 | bytes 65536 | tf_op jit(solution)/shard_map/while/body/eval_jaxpr/psum | solution.py:86
  864.4 5.8 all_gather.43
  871.9 5.2 all_gather.45
  880.0 5.2 all_gather.44
  885.8 4.7 fusion.54
  890.4 11.2 %psum.25 = f32[16,512]{1,0:T(8,128)S(1)} all-reduce(f32[16,512]{1,0:T(8,128)S(1)} %fusion.54), channel_id=1, replica_groups=mesh['groups'=2,'tensor'=4,'section'=4] {'tensor'}, use_global_device_ids=true, to_apply=%region_2.2 | all-reduce | flops 8192 | bytes 65536 | tf_op jit(solution)/shard_map/while/body/eval_jaxpr/psum | solution.py:86
  910.7 5.8 all_gather.43
  918.2 5.2 all_gather.45
  926.3 5.2 all_gather.44
  932.1 4.7 fusion.54
  936.7 11.0 %psum.25 = f32[16,512]{1,0:T(8,128)S(1)} all-reduce(f32[16,512]{1,0:T(8,128)S(1)} %fusion.54), channel_id=1, replica_groups=mesh['groups'=2,'tensor'=4,'section'=4] {'tensor'}, use_global_device_ids=true, to_apply=%region_2.2 | all-reduce | flops 8192 | bytes 65536 | tf_op jit(solution)/shard_map/while/body/eval_jaxpr/psum | solution.py:86
  957.5 37.0 %all-reduce.2.cloned.1.call-done = bf16[64,2048]{1,0:T(8,128)(2,1)} async-done(((bf16[64,2048]{1,0:T(8,128)(2,1)}), bf16[64,2048]{1,0:T(8,128)(2,1)}) %all-reduce.2.cloned.1.call-update) | async-done | bytes 262160 | tf_op jit(solution)/shard_map/psum | solution.py:17
  (137 shorter events, 114.8 us)
Async XLA Ops:
  13.4 48.0 %all-to-all-start.1 = ((bf16[4,128,3584]{1,0,2:T(4,128)(2,1)}), bf16[4,128,3584]{1,0,2:T(4,128)(2,1)}, u32[]{:S(2)}, u32[]{:S(2)}) async-start(bf16[4,128,3584]{1,0,2:T(4,128)(2,1)} %copy.26), calls=%async_computation.1 | async-start | bytes 7340032 | tf_op jit(solution)/shard_map/all_to_all | solution.py:39
  61.4 47.4 %all-to-all-start.4 = ((bf16[4,128,3584]{1,0,2:T(4,128)(2,1)}), bf16[4,128,3584]{1,0,2:T(4,128)(2,1)}, u32[]{:S(2)}, u32[]{:S(2)}) async-start(bf16[4,128,3584]{1,0,2:T(4,128)(2,1)} %copy.30), calls=%async_computation.4 | async-start | bytes 7340032 | tf_op jit(solution)/shard_map/all_to_all | solution.py:46
  73.0 83.9 %copy-start.6 = (bf16[4,128,2048]{2,1,0:T(8,128)(2,1)S(1)}, bf16[4,128,2048]{2,1,0:T(8,128)(2,1)}, u32[]{:S(2)}) copy-start(bf16[4,128,2048]{2,1,0:T(8,128)(2,1)} %param.14) | copy-start | bytes 6291460
  156.9 53.6 %copy-start.7 = (bf16[4,128,2048]{2,1,0:T(8,128)(2,1)S(1)}, bf16[4,128,2048]{2,1,0:T(8,128)(2,1)}, u32[]{:S(2)}) copy-start(bf16[4,128,2048]{2,1,0:T(8,128)(2,1)} %param.15) | copy-start | bytes 6291460
  260.9 50.9 %all-to-all-start.8 = ((bf16[4,2048,128]{2,1,0:T(8,128)(2,1)}), bf16[4,2048,128]{2,1,0:T(8,128)(2,1)S(1)}, u32[]{:S(2)}, u32[]{:S(2)}) async-start(bf16[4,2048,128]{2,1,0:T(8,128)(2,1)} %param.19), calls=%async_computation.8 | async-start | bytes 4194304 | tf_op jit(solution)/shard_map/all_to_all | solution.py:35
  311.8 1.3 copy-start.1
  313.1 86.2 %all-to-all-start.2 = ((bf16[4,512,896]{2,1,0:T(8,128)(2,1)}), bf16[4,512,896]{2,1,0:T(8,128)(2,1)}, u32[]{:S(2)}, u32[]{:S(2)}) async-start(bf16[4,512,896]{2,1,0:T(8,128)(2,1)} %bitcast.83), calls=%async_computation.2 | async-start | bytes 7340032 | tf_op jit(solution)/shard_map/all_to_all | solution.py:38
  399.4 86.2 %all-to-all-start.5 = ((bf16[4,512,896]{2,1,0:T(8,128)(2,1)}), bf16[4,512,896]{2,1,0:T(8,128)(2,1)}, u32[]{:S(2)}, u32[]{:S(2)}) async-start(bf16[4,512,896]{2,1,0:T(8,128)(2,1)} %bitcast.82), calls=%async_computation.5 | async-start | bytes 7340032 | tf_op jit(solution)/shard_map/all_to_all | solution.py:45
  485.6 5.0 copy-start.8
  485.6 94.0 %copy-start.9 = (s32[1,3]{1,0:T(1,128)S(1)}, s32[1,3]{1,0:T(1,128)}, u32[]{:S(2)}) copy-start(s32[1,3]{1,0:T(1,128)} %param.13) | copy-start | bytes 40
  485.6 94.6 %copy-start.4 = (bf16[4,128,2048]{2,1,0:T(8,128)(2,1)S(1)}, bf16[4,128,2048]{2,1,0:T(8,128)(2,1)}, u32[]{:S(2)}) copy-start(bf16[4,128,2048]{2,1,0:T(8,128)(2,1)} %all_to_all.145) | copy-start | bytes 6291460
  485.6 137.3 %all-to-all-start.7 = ((bf16[4,512,896]{2,1,0:T(8,128)(2,1)}), bf16[4,512,896]{2,1,0:T(8,128)(2,1)}, u32[]{:S(2)}, u32[]{:S(2)}) async-start(bf16[4,512,896]{2,1,0:T(8,128)(2,1)} %bitcast.80), calls=%async_computation.7 | async-start | bytes 7340032 | tf_op jit(solution)/shard_map/all_to_all | solution.py:52
  490.5 504.0 %all-reduce.2.cloned.1.call-start = ((), (), s32[]{:S(2)}) async-start(), calls=%async_computation.9 | async-start | bytes 524288 | tf_op jit(solution)/shard_map/psum | solution.py:17
  580.2 3.1 copy-start.3
  583.3 4.4 copy-start.2
  628.9 6.0 copy-start.5
  641.0 14.8 %copy-start = (bf16[512,3584]{1,0:T(8,128)(2,1)S(1)}, bf16[512,3584]{1,0:T(8,128)(2,1)}, u32[]{:S(2)}) copy-start(bf16[512,3584]{1,0:T(8,128)(2,1)} %get-tuple-element.710) | copy-start | bytes 11010052 | tf_op jit(solution)/shard_map/while
  674.9 4.8 collective-permute-start
  685.7 14.8 %copy-start = (bf16[512,3584]{1,0:T(8,128)(2,1)S(1)}, bf16[512,3584]{1,0:T(8,128)(2,1)}, u32[]{:S(2)}) copy-start(bf16[512,3584]{1,0:T(8,128)(2,1)} %get-tuple-element.710) | copy-start | bytes 11010052 | tf_op jit(solution)/shard_map/while
  719.8 6.2 collective-permute-start
  732.0 14.8 %copy-start = (bf16[512,3584]{1,0:T(8,128)(2,1)S(1)}, bf16[512,3584]{1,0:T(8,128)(2,1)}, u32[]{:S(2)}) copy-start(bf16[512,3584]{1,0:T(8,128)(2,1)} %get-tuple-element.710) | copy-start | bytes 11010052 | tf_op jit(solution)/shard_map/while
  765.8 6.2 collective-permute-start
  778.1 14.8 %copy-start = (bf16[512,3584]{1,0:T(8,128)(2,1)S(1)}, bf16[512,3584]{1,0:T(8,128)(2,1)}, u32[]{:S(2)}) copy-start(bf16[512,3584]{1,0:T(8,128)(2,1)} %get-tuple-element.710) | copy-start | bytes 11010052 | tf_op jit(solution)/shard_map/while
  812.1 6.2 collective-permute-start
  824.4 14.8 %copy-start = (bf16[512,3584]{1,0:T(8,128)(2,1)S(1)}, bf16[512,3584]{1,0:T(8,128)(2,1)}, u32[]{:S(2)}) copy-start(bf16[512,3584]{1,0:T(8,128)(2,1)} %get-tuple-element.710) | copy-start | bytes 11010052 | tf_op jit(solution)/shard_map/while
  858.2 6.2 collective-permute-start
  870.4 14.8 %copy-start = (bf16[512,3584]{1,0:T(8,128)(2,1)S(1)}, bf16[512,3584]{1,0:T(8,128)(2,1)}, u32[]{:S(2)}) copy-start(bf16[512,3584]{1,0:T(8,128)(2,1)} %get-tuple-element.710) | copy-start | bytes 11010052 | tf_op jit(solution)/shard_map/while
  904.5 6.2 collective-permute-start
  916.7 14.8 %copy-start = (bf16[512,3584]{1,0:T(8,128)(2,1)S(1)}, bf16[512,3584]{1,0:T(8,128)(2,1)}, u32[]{:S(2)}) copy-start(bf16[512,3584]{1,0:T(8,128)(2,1)} %get-tuple-element.710) | copy-start | bytes 11010052 | tf_op jit(solution)/shard_map/while
  950.6 6.2 collective-permute-start
Sparse Core Ops, SparseCore 0:
  957.6 36.8 all-reduce.1
where the time goes:
time: 1010 us; the launch traced here: 1000 us
  blocking collectives  432 us (43%)
  waiting for transfers between devices  312 us (31%)
  local copies, waits for them, and re-layouts  99.4 us (10%)
  matrix products  73.3 us (7%)
  starting transfers between devices  56.1 us (6%)
  other arithmetic  16.3 us (2%)
  between operations  13.5 us (1%)
    all_gather x1, blocking collectives, body(): prompt_rows = lax.all_gather(prompt, 'section', axis=0, tiled=True)  89 us
    psum x7, blocking collectives, layer_step(): summed = lax.psum(contract_last(hidden, down_rows), 'tensor')  77.6 us
    all_to_all x1, waiting for transfers between devices, body(): lax.all_to_all(lax.all_to_all(gate_right, 'tensor', split_axis=2, concat_...  74.6 us
    all_to_all x1, waiting for transfers between devices, body(): lax.all_to_all(lax.all_to_all(up_right, 'tensor', split_axis=2, concat_ax...  74.5 us
    dot_general x28, matrix products, contract_last(): lax.dot_general(left_side, right_side, (((1,), (1,)), ((), ())), preferre...  69.2 us
    all_to_all x1, blocking collectives, body(): lax.all_to_all(gate_left, 'section', split_axis=0, concat_axis=2, tiled=T...  53.6 us
    all_to_all x1, blocking collectives, body(): lax.all_to_all(up_left, 'section', split_axis=0, concat_axis=2, tiled=True)  50.5 us
    all_to_all x1, blocking collectives, body(): lax.all_to_all(down_left, 'tensor', split_axis=2, concat_axis=1, tiled=True)  48.1 us
  transfers between devices with their start and end apart: 14, of which 13 were waited for; matrix products, arithmetic and copies ran while one was open for 8% of the time, Pallas kernels for 0%

commit v1 on v0

v1 whole, which is shorter than its diff:
```python
import functools

import jax
import jax.numpy as jnp
from jax import lax
from jax.experimental import pallas as pl
from jax.experimental.pallas import tpu as pltpu
from jax.sharding import PartitionSpec as P

BF16, F32 = jnp.bfloat16, jnp.float32
AUX, SPREAD, GATE_SUM, GATE_ALL, HID_SUM, HID_ALL, DOWN_SUM, DOWN_ALL, OUT_SUM = range(9)


def contract_last(left_side, right_side):
    return lax.dot_general(
        left_side, right_side, (((1,), (1,)), ((), ())), preferred_element_type=F32
    )


def kernel(
    nt, ns, features,
    prompt, norm_gain, kept, gl_hbm, ul_hbm, gr_hbm, ur_hbm, dl_hbm, dr_hbm,
    out,
    gl, ul, gr, ur, dl, dr,
    gain_out, gain, mask_out, mask,
    own, wide, low_out, low_in, low, val_out, val_in, hid, down_out, down_in,
    dlow_own, dlow, br_out, br_in,
    send, recv, mask_send, mask_recv, load,
):
    t, s = lax.axis_index("tensor"), lax.axis_index("section")
    layers = gl.shape[0]
    fan = nt // ns
    rows, f_block = own.shape
    span = rows * ns
    slab = hid.shape[1]
    rank = gl.shape[1]
    home, part = lax.div(t, fan), lax.rem(t, fan)

    def loads(l):
        return [
            pltpu.make_async_copy(h.at[l], v.at[l], load.at[i, l])
            for i, (h, v) in enumerate(
                ((gl_hbm, gl), (ul_hbm, ul), (gr_hbm, gr), (ur_hbm, ur), (dl_hbm, dl), (dr_hbm, dr))
            )
        ]

    def start_loads(l, carry):
        for copy in loads(l):
            copy.start()
        return carry

    lax.fori_loop(0, layers, start_loads, 0)

    count = nt * ns
    me = t * ns + s
    barrier = pltpu.get_barrier_semaphore()

    def greet(j, carry):
        peer = lax.rem(me + j, count)
        pl.semaphore_signal(
            barrier, inc=1,
            device_id={"tensor": lax.div(peer, ns), "section": lax.rem(peer, ns)},
            device_id_type=pl.DeviceIdType.MESH,
        )
        return carry

    lax.fori_loop(1, count, greet, 0)

    for j in range(ns):
        for kk in range(fan):
            at = (j * fan + kk) * f_block
            gain_out[j, kk] = norm_gain[:, at:at + f_block]
    position = t * rank + lax.broadcasted_iota(jnp.int32, (1, rank), 1)
    for i in range(3):
        mask_out[i] = jnp.where(position < kept[0, i], 1.0, 0.0).astype(F32)
    own[...] = prompt[...]
    pl.semaphore_wait(barrier, count - 1)

    def copy_to(phase, src, dst, dest_slot, src_slot, tt, ss, sems=None):
        sender, receiver = (send, recv) if sems is None else sems
        return pltpu.make_async_remote_copy(
            src_ref=src, dst_ref=dst,
            send_sem=sender.at[phase, dest_slot], recv_sem=receiver.at[phase, src_slot],
            device_id={"tensor": tt, "section": ss}, device_id_type=pl.DeviceIdType.MESH,
        )

    def over_section(phase, src_of, dst_of, sems=None):
        sends, recvs = [], []
        for j in range(1, ns):
            peer = lax.rem(s + j, ns)
            sends.append(copy_to(phase, src_of(peer), dst_of(s), peer, s, t, peer, sems))
            recvs.append(copy_to(phase, src_of(peer), dst_of(peer), peer, peer, t, peer, sems))
        return sends, recvs

    def over_tensor(phase, src_of, dst_of):
        sends, recvs = [], []
        for j in range(1, nt):
            peer = lax.rem(t + j, nt)
            sends.append(copy_to(phase, src_of(peer), dst_of(t), peer, t, peer, s))
            recvs.append(copy_to(phase, src_of(peer), dst_of(peer), peer, peer, peer, s))
        return sends, recvs

    def start(copies):
        for copy in copies:
            copy.start()

    def wait_recv(copies):
        for copy in copies:
            copy.wait_recv()

    def wait_send(copies):
        for copy in copies:
            copy.wait_send()

    def spread(phase, src, dst):
        is_home = home == s

        def each(action):
            for j in range(nt):
                peer = lax.rem(t + j, nt)
                copy = copy_to(phase, src, dst.at[s, part], peer, s * fan + part, peer, home)
                if j == 0:
                    @pl.when(jnp.logical_not(is_home))
                    def _():
                        action(copy)
                else:
                    action(copy)

        def begin():
            each(lambda copy: copy.start())

            @pl.when(is_home)
            def _():
                dst[s, part] = src[...]

        def arrive():
            for j in range(ns):
                for kk in range(fan):
                    copy = copy_to(phase, src, dst.at[j, kk], 0, j * fan + kk, s * fan + kk, j)

                    @pl.when(jnp.logical_not((s * fan + kk == t) & (s == j)))
                    def _():
                        copy.wait_recv()

        def finish():
            each(lambda copy: copy.wait_send())

        return begin, arrive, finish

    gain_send, gain_recv = over_section(AUX, lambda j: gain_out.at[j], lambda j: gain.at[j])
    mask_sends, mask_recvs = over_section(
        0, lambda j: mask_out, lambda j: mask.at[j], (mask_send, mask_recv)
    )
    aux_first = spread(SPREAD, own, wide)
    low_sum = over_section(GATE_SUM, lambda j: low_out.at[j], lambda j: low_in.at[j])
    low_all = over_section(GATE_ALL, lambda j: low.at[s], lambda j: low.at[j])
    hid_sum = over_tensor(HID_SUM, lambda j: val_out.at[j], lambda j: val_in.at[j])
    hid_all = over_tensor(HID_ALL, lambda j: hid.at[t], lambda j: hid.at[j])
    down_sum = over_section(DOWN_SUM, lambda j: down_out.at[j], lambda j: down_in.at[j])
    down_all = spread(DOWN_ALL, dlow_own, dlow)
    out_sum = over_section(OUT_SUM, lambda j: br_out.at[j], lambda j: br_in.at[j])

    start(gain_send)
    start(mask_sends)
    gain[s] = gain_out[s]
    mask[s] = mask_out[...]

    def layer(l, carry):
        begin, arrive, finish = aux_first
        begin()

        @pl.when(l == 0)
        def _():
            wait_recv(gain_recv)
            wait_recv(mask_recvs)

        weights = loads(l)
        weights[0].wait()
        weights[1].wait()
        arrive()

        gate_part = jnp.zeros((span, rank), F32)
        up_part = jnp.zeros((span, rank), F32)
        squares = jnp.zeros((span, 1), F32)
        for kk in range(fan):
            piece = wide[:, kk].reshape(span, f_block).astype(F32)
            squares += jnp.sum(piece * piece, axis=-1, keepdims=True)
            scaled = (piece * gain[l, kk]).astype(BF16)
            at = kk * f_block
            gate_part += contract_last(scaled, gl[l, :, at:at + f_block])
            up_part += contract_last(scaled, ul[l, :, at:at + f_block])
        low_out[:, 0] = gate_part.reshape(ns, rows, rank)
        low_out[:, 1] = up_part.reshape(ns, rows, rank)
        low_out[:, 2] = jnp.broadcast_to(squares, (span, rank)).reshape(ns, rows, rank)
        start(low_sum[0])
        low_in[s] = low_out[s]
        wait_recv(low_sum[1])
        total = jnp.sum(low_in[...], axis=0)
        scale = lax.rsqrt(total[2] / features + 1e-05)
        low[s, 0] = (total[0] * scale * mask[l, 0]).astype(BF16)
        low[s, 1] = (total[1] * scale * mask[l, 1]).astype(BF16)
        start(low_all[0])
        weights[2].wait()
        weights[3].wait()
        wait_recv(low_all[1])

        width = gr.shape[2]
        gate_low = low[:, 0].reshape(span, rank)
        up_low = low[:, 1].reshape(span, rank)
        gate_values = jnp.dot(gate_low, gr[l], preferred_element_type=F32)
        val_out[:, 0] = gate_values.astype(BF16).reshape(nt, slab, width)
        up_values = jnp.dot(up_low, ur[l], preferred_element_type=F32)
        val_out[:, 1] = up_values.astype(BF16).reshape(nt, slab, width)
        start(hid_sum[0])
        val_in[t] = val_out[t]
        wait_recv(hid_sum[1])
        gate_sum = jnp.sum(val_in[:, 0].astype(F32), axis=0)
        up_sum = jnp.sum(val_in[:, 1].astype(F32), axis=0)
        hid[t] = (gate_sum / (1.0 + jnp.exp(-gate_sum)) * up_sum).astype(BF16)
        start(hid_all[0])
        weights[4].wait()
        wait_recv(hid_all[1])

        down_out[...] = contract_last(hid[...].reshape(span, width), dl[l]).reshape(ns, rows, rank)
        start(down_sum[0])
        down_in[s] = down_out[s]
        wait_recv(down_sum[1])
        dlow_own[...] = (jnp.sum(down_in[...], axis=0) * mask[l, 2]).astype(BF16)
        begin_down, arrive_down, finish_down = down_all
        begin_down()
        weights[5].wait()
        arrive_down()

        branch = jnp.zeros((span, f_block), F32)
        for kk in range(fan):
            at = kk * rank
            branch += contract_last(dlow[:, kk].reshape(span, rank), dr[l, :, at:at + rank])
        br_out[...] = branch.astype(BF16).reshape(ns, rows, f_block)
        start(out_sum[0])
        br_in[s] = br_out[s]
        wait_recv(out_sum[1])
        finish()
        own[...] = (own[...].astype(F32) + jnp.sum(br_in[...].astype(F32), axis=0)).astype(BF16)

        wait_send(low_sum[0])
        wait_send(low_all[0])
        wait_send(hid_sum[0])
        wait_send(hid_all[0])
        wait_send(down_sum[0])
        finish_down()
        wait_send(out_sum[0])
        return carry

    lax.fori_loop(0, layers, layer, 0)
    wait_send(gain_send)
    wait_send(mask_sends)
    out[...] = own[...]


def body(
    nt, ns,
    prompt, norm_gain, kept_ranks, gate_left, up_left, gate_right, up_right, down_left, down_right,
):
    rows, f_block = prompt.shape
    layers, rank, _ = gate_left.shape
    width = gate_right.shape[2]
    fan = nt // ns
    span = rows * ns
    slab = span // nt
    slots = max(nt, ns, ns * fan)
    weights = (gate_left, up_left, gate_right, up_right, down_left, down_right)
    vmem, hbm = pl.BlockSpec(memory_space=pltpu.VMEM), pl.BlockSpec(memory_space=pl.ANY)
    return pl.pallas_call(
        functools.partial(kernel, nt, ns, float(norm_gain.shape[1])),
        out_shape=jax.ShapeDtypeStruct((rows, f_block), BF16),
        in_specs=[vmem, vmem, pl.BlockSpec(memory_space=pltpu.SMEM)] + [hbm] * 6,
        out_specs=vmem,
        scratch_shapes=[pltpu.VMEM(w.shape, BF16) for w in weights] + [
            pltpu.VMEM((ns, fan, 1, f_block), F32),
            pltpu.VMEM((ns, fan, 1, f_block), F32),
            pltpu.VMEM((3, 1, rank), F32),
            pltpu.VMEM((ns, 3, 1, rank), F32),
            pltpu.VMEM((rows, f_block), BF16),
            pltpu.VMEM((ns, fan, rows, f_block), BF16),
            pltpu.VMEM((ns, 3, rows, rank), F32),
            pltpu.VMEM((ns, 3, rows, rank), F32),
            pltpu.VMEM((ns, 2, rows, rank), BF16),
            pltpu.VMEM((nt, 2, slab, width), BF16),
            pltpu.VMEM((nt, 2, slab, width), BF16),
            pltpu.VMEM((nt, slab, width), BF16),
            pltpu.VMEM((ns, rows, rank), F32),
            pltpu.VMEM((ns, rows, rank), F32),
            pltpu.VMEM((rows, rank), BF16),
            pltpu.VMEM((ns, fan, rows, rank), BF16),
            pltpu.VMEM((ns, rows, f_block), BF16),
            pltpu.VMEM((ns, rows, f_block), BF16),
            pltpu.SemaphoreType.DMA((9, slots)),
            pltpu.SemaphoreType.DMA((9, slots)),
            pltpu.SemaphoreType.DMA((1, slots)),
            pltpu.SemaphoreType.DMA((1, slots)),
            pltpu.SemaphoreType.DMA((6, layers)),
        ],
        compiler_params=pltpu.CompilerParams(
            collective_id=0, has_side_effects=True, vmem_limit_bytes=52 * 1024 * 1024
        ),
        cost_estimate=pl.CostEstimate(
            flops=2 * span * sum(w.size for w in weights),
            bytes_accessed=2 * sum(w.size for w in weights),
            transcendentals=span * width * layers // nt,
        ),
    )(prompt, norm_gain, kept_ranks, *weights)


def solution(mesh):
    in_specs = (
        P(("groups", "section"), "tensor"),
        P(("groups", "section"), None),
        P(("groups", "section"), None),
    ) + (P("groups", "tensor", "section"),) * 6
    return jax.shard_map(
        functools.partial(body, mesh.shape["tensor"], mesh.shape["section"]),
        mesh=mesh, in_specs=in_specs, out_specs=P(("groups", "section"), "tensor"), check_vma=False,
    )
```

time: 1010 us -> 215 us (0.21)
  blocking collectives: 432 us -> 0 us
  waiting for transfers between devices: 312 us -> 0 us
  Pallas kernels: 0 us -> 212 us
  local copies, waits for them, and re-layouts: 99.4 us -> 2.88 us
  matrix products: 73.3 us -> 0 us
  starting transfers between devices: 56.1 us -> 0 us
  other arithmetic: 16.3 us -> 0 us
  between operations: 13.5 us -> 0.01 us
    all_to_all x6 -> x0, waiting for transfers between devices: 262 us -> none  [the longest x1 74.6 us: body(): lax.all_to_all(lax.all_to_all(gate_right, 'tensor', split_axis=2, concat_...]
    pallas_call x0 -> x1, Pallas kernels: none -> 212 us  [body(): pl.pallas_call(functools.partial(kernel, nt, ns, float(norm_gain.shape[1]...]
    all_gather x22 -> x0, blocking collectives: 202 us -> none  [the longest x1 89 us: body(): prompt_rows = lax.all_gather(prompt, 'section', axis=0, tiled=True)]
    all_to_all x3 -> x0, blocking collectives: 152 us -> none  [the longest x1 53.6 us: body(): lax.all_to_all(gate_left, 'section', split_axis=0, concat_axis=2, tiled=T...]
    psum x7 -> x0, blocking collectives: 77.6 us -> none  [layer_step(): summed = lax.psum(contract_last(hidden, down_rows), 'tensor')]
    dot_general x35 -> x0, matrix products: 73.3 us -> none  [the longest x28 69.2 us: contract_last(): lax.dot_general(left_side, right_side, (((1,), (1,)), ((), ())), preferre...]
    all_to_all x9 -> x0, local copies, waits for them, and re-layouts: 51.6 us -> none  [the longest x1 9.73 us: body(): lax.all_to_all(down_right, 'section', split_axis=0, concat_axis=2, tiled=...]
    unnamed x27 -> x7, local copies, waits for them, and re-layouts: 45.7 us -> 2.88 us
  transfers between devices with their start and end apart: 14 -> 0, of which waited for: 13 -> 0; matrix products, arithmetic and copies ran while one was open for 8% -> 0% of each run, Pallas kernels for 0% -> 0%
where the time goes in v1:
time: 215 us
  Pallas kernels  212 us (99%)
  local copies, waits for them, and re-layouts  2.88 us (1%)
    pallas_call x1, Pallas kernels, body(): pl.pallas_call(functools.partial(kernel, nt, ns, float(norm_gain.shape[1]...  212 us

profile of v1, /device:TPU:0, one launch (start us, length us, event | category | flops | bytes accessed | tf_op | source)
XLA Modules:
  0.0 214.5 jit_solution(14079016662776987678)
XLA Ops:
  0.0 0.0 copy-start
  0.0 0.8 copy-done
  0.8 0.0 copy-start.1
  0.8 0.8 copy-done.1
  1.6 0.0 copy-start.2
  1.6 0.7 copy-done.2
  2.3 211.6 %shard_map.91 = bf16[16,2048]{1,0:T(8,128)(2,1)S(1)} custom-call(bf16[16,2048]{1,0:T(8,128)(2,1)S(1)} %copy-done, f32[1,8192]{1,0:T(1,128)S(1)} %copy-done.1, s32[1,3]{1,0:T(1,128)S(1)} %copy-done.2, bf16[4,128,2048]{2,1,0:T(8,128)(2,1)} %gl_hbm.1, bf16[4,128,2048]{2,1,0:T(8,128)(2,1)} %ul_hbm.1, bf16[4,128,3584]{2,1,0:T(8,128)(2,1)} %gr_hbm.1, ...), custom_call_target="tpu_custom_call" | custom-call | flops 1107296256 | bytes 17301504 | tf_op jit(solution)/shard_map/pallas_call | solution.py:273
  213.9 0.6 copy.11
Async XLA Ops:
  0.0 0.8 copy-start
  0.8 0.8 copy-start.1
  1.6 0.7 copy-start.2

commit v2 on v1

--- a/solution.py
+++ b/solution.py
@@ -8,7 +8,8 @@
 from jax.sharding import PartitionSpec as P
 
 BF16, F32 = jnp.bfloat16, jnp.float32
-AUX, SPREAD, GATE_SUM, GATE_ALL, HID_SUM, HID_ALL, DOWN_SUM, DOWN_ALL, OUT_SUM = range(9)
+AUX, SPREAD, GATHER, GATE_SUM, GATE_ALL, PAIR, GATE_VALUES, UP_VALUES = range(8)
+HID_ALL, DOWN_SUM, DOWN_ALL, OUT_SUM, PHASES = range(8, 13)
 
 
 def contract_last(left_side, right_side):
@@ -23,18 +24,22 @@
     out,
     gl, ul, gr, ur, dl, dr,
     gain_out, gain, mask_out, mask,
-    own, wide, low_out, low_in, low, val_out, val_in, hid, down_out, down_in,
+    own, wide, low_out, low_in, low, val_out, pair_in, val_mid, val_in, hid, down_out, down_in,
     dlow_own, dlow, br_out, br_in,
     send, recv, mask_send, mask_recv, load,
 ):
     t, s = lax.axis_index("tensor"), lax.axis_index("section")
     layers = gl.shape[0]
     fan = nt // ns
-    rows, f_block = own.shape
+    _, rows, piece = own.shape
+    f_block = piece * nt
     span = rows * ns
     slab = hid.shape[1]
     rank = gl.shape[1]
     home, part = lax.div(t, fan), lax.rem(t, fan)
+    chips = nt // 2
+    chip, core = lax.div(t, 2), lax.rem(t, 2)
+    sibling = chip * 2 + 1 - core
 
     def loads(l):
         return [
@@ -73,7 +78,8 @@
     position = t * rank + lax.broadcasted_iota(jnp.int32, (1, rank), 1)
     for i in range(3):
         mask_out[i] = jnp.where(position < kept[0, i], 1.0, 0.0).astype(F32)
-    own[...] = prompt[...]
+    for p in range(nt):
+        own[p] = prompt[:, p * piece:(p + 1) * piece]
     pl.semaphore_wait(barrier, count - 1)
 
     def copy_to(phase, src, dst, dest_slot, src_slot, tt, ss, sems=None):
@@ -100,6 +106,18 @@
             recvs.append(copy_to(phase, src_of(peer), dst_of(peer), peer, peer, peer, s))
         return sends, recvs
 
+    def pair_copies(i):
+        return copy_to(PAIR, val_out.at[i, 1 - core], pair_in.at[i], i, i, sibling, s)
+
+    def over_chips(phase, i):
+        sends, recvs = [], []
+        for j in range(1, chips):
+            peer = lax.rem(chip + j, chips)
+            src, to = val_mid.at[i, peer], peer * 2 + core
+            sends.append(copy_to(phase, src, val_in.at[i, chip], peer, chip, to, s))
+            recvs.append(copy_to(phase, src, val_in.at[i, peer], peer, peer, to, s))
+        return sends, recvs
+
     def start(copies):
         for copy in copies:
             copy.start()
@@ -112,13 +130,15 @@
         for copy in copies:
             copy.wait_send()
 
-    def spread(phase, src, dst):
+    def spread(phase, src_of, dst_of):
         is_home = home == s
 
         def each(action):
             for j in range(nt):
                 peer = lax.rem(t + j, nt)
-                copy = copy_to(phase, src, dst.at[s, part], peer, s * fan + part, peer, home)
+                copy = copy_to(
+                    phase, src_of(peer), dst_of(peer).at[s, part], peer, s * fan + part, peer, home
+                )
                 if j == 0:
                     @pl.when(jnp.logical_not(is_home))
                     def _():
@@ -131,12 +151,14 @@
 
             @pl.when(is_home)
             def _():
-                dst[s, part] = src[...]
+                dst_of(t)[s, part] = src_of(t)[...]
 
         def arrive():
             for j in range(ns):
                 for kk in range(fan):
-                    copy = copy_to(phase, src, dst.at[j, kk], 0, j * fan + kk, s * fan + kk, j)
+                    copy = copy_to(
+                        phase, src_of(t), dst_of(t).at[j, kk], 0, j * fan + kk, s * fan + kk, j
+                    )
 
                     @pl.when(jnp.logical_not((s * fan + kk == t) & (s == j)))
                     def _():
@@ -151,13 +173,15 @@
     mask_sends, mask_recvs = over_section(
         0, lambda j: mask_out, lambda j: mask.at[j], (mask_send, mask_recv)
     )
-    aux_first = spread(SPREAD, own, wide)
+    aux_first = spread(SPREAD, lambda j: own.at[j], lambda j: wide.at[j])
+    gather = over_tensor(GATHER, lambda j: wide.at[t], lambda j: wide.at[j])
     low_sum = over_section(GATE_SUM, lambda j: low_out.at[j], lambda j: low_in.at[j])
     low_all = over_section(GATE_ALL, lambda j: low.at[s], lambda j: low.at[j])
-    hid_sum = over_tensor(HID_SUM, lambda j: val_out.at[j], lambda j: val_in.at[j])
+    pairs = [pair_copies(i) for i in range(2)]
+    values = [over_chips(GATE_VALUES, 0), over_chips(UP_VALUES, 1)]
     hid_all = over_tensor(HID_ALL, lambda j: hid.at[t], lambda j: hid.at[j])
     down_sum = over_section(DOWN_SUM, lambda j: down_out.at[j], lambda j: down_in.at[j])
-    down_all = spread(DOWN_ALL, dlow_own, dlow)
+    down_all = spread(DOWN_ALL, lambda j: dlow_own, lambda j: dlow)
     out_sum = over_section(OUT_SUM, lambda j: br_out.at[j], lambda j: br_in.at[j])
 
     start(gain_send)
@@ -179,23 +203,27 @@
         weights[1].wait()
         arrive()
 
+        start(gather[0])
         gate_part = jnp.zeros((span, rank), F32)
         up_part = jnp.zeros((span, rank), F32)
         squares = jnp.zeros((span, 1), F32)
-        for kk in range(fan):
-            piece = wide[:, kk].reshape(span, f_block).astype(F32)
-            squares += jnp.sum(piece * piece, axis=-1, keepdims=True)
-            scaled = (piece * gain[l, kk]).astype(BF16)
-            at = kk * f_block
-            gate_part += contract_last(scaled, gl[l, :, at:at + f_block])
-            up_part += contract_last(scaled, ul[l, :, at:at + f_block])
-        low_out[:, 0] = gate_part.reshape(ns, rows, rank)
-        low_out[:, 1] = up_part.reshape(ns, rows, rank)
-        low_out[:, 2] = jnp.broadcast_to(squares, (span, rank)).reshape(ns, rows, rank)
+        wait_recv(gather[1])
+        for p in range(nt):
+            for kk in range(fan):
+                values_here = wide[p, :, kk].reshape(span, piece).astype(F32)
+                squares += jnp.sum(values_here * values_here, axis=-1, keepdims=True)
+                at = kk * f_block + p * piece
+                gains = gain[l, kk, :, p * piece:(p + 1) * piece]
+                scaled = (values_here * gains).astype(BF16)
+                gate_part += contract_last(scaled, gl[l, :, at:at + piece])
+                up_part += contract_last(scaled, ul[l, :, at:at + piece])
+        low_out[:, 0] = gate_part.astype(BF16).reshape(ns, rows, rank)
+        low_out[:, 1] = up_part.astype(BF16).reshape(ns, rows, rank)
+        low_out[:, 2] = jnp.broadcast_to(squares, (span, rank)).astype(BF16).reshape(ns, rows, rank)
         start(low_sum[0])
         low_in[s] = low_out[s]
         wait_recv(low_sum[1])
-        total = jnp.sum(low_in[...], axis=0)
+        total = jnp.sum(low_in[...].astype(F32), axis=0)
         scale = lax.rsqrt(total[2] / features + 1e-05)
         low[s, 0] = (total[0] * scale * mask[l, 0]).astype(BF16)
         low[s, 1] = (total[1] * scale * mask[l, 1]).astype(BF16)
@@ -207,25 +235,37 @@
         width = gr.shape[2]
         gate_low = low[:, 0].reshape(span, rank)
         up_low = low[:, 1].reshape(span, rank)
-        gate_values = jnp.dot(gate_low, gr[l], preferred_element_type=F32)
-        val_out[:, 0] = gate_values.astype(BF16).reshape(nt, slab, width)
-        up_values = jnp.dot(up_low, ur[l], preferred_element_type=F32)
-        val_out[:, 1] = up_values.astype(BF16).reshape(nt, slab, width)
-        start(hid_sum[0])
-        val_in[t] = val_out[t]
-        wait_recv(hid_sum[1])
-        gate_sum = jnp.sum(val_in[:, 0].astype(F32), axis=0)
-        up_sum = jnp.sum(val_in[:, 1].astype(F32), axis=0)
+        wait_send(gather[0])
+        for i, (narrow, right) in enumerate(((gate_low, gr), (up_low, ur))):
+            product = jnp.dot(narrow, right[l], preferred_element_type=F32).astype(BF16)
+            for j in range(nt):
+                val_out[i, j % 2, j // 2] = product[j * slab:(j + 1) * slab]
+            pairs[i].start()
+        sums = []
+        for i in range(2):
+            pairs[i].wait_recv()
+            for j in range(chips):
+                val_mid[i, j] = (
+                    val_out[i, core, j].astype(F32) + pair_in[i, j].astype(F32)
+                ).astype(BF16)
+            start(values[i][0])
+            val_in[i, chip] = val_mid[i, chip]
+        for i in range(2):
+            wait_recv(values[i][1])
+            sums.append(jnp.sum(val_in[i].astype(F32), axis=0))
+        gate_sum, up_sum = sums
         hid[t] = (gate_sum / (1.0 + jnp.exp(-gate_sum)) * up_sum).astype(BF16)
         start(hid_all[0])
         weights[4].wait()
         wait_recv(hid_all[1])
 
-        down_out[...] = contract_last(hid[...].reshape(span, width), dl[l]).reshape(ns, rows, rank)
+        down_out[...] = contract_last(
+            hid[...].reshape(span, width), dl[l]
+        ).astype(BF16).reshape(ns, rows, rank)
         start(down_sum[0])
         down_in[s] = down_out[s]
         wait_recv(down_sum[1])
-        dlow_own[...] = (jnp.sum(down_in[...], axis=0) * mask[l, 2]).astype(BF16)
+        dlow_own[...] = (jnp.sum(down_in[...].astype(F32), axis=0) * mask[l, 2]).astype(BF16)
         begin_down, arrive_down, finish_down = down_all
         begin_down()
         weights[5].wait()
@@ -240,11 +280,15 @@
         br_in[s] = br_out[s]
         wait_recv(out_sum[1])
         finish()
-        own[...] = (own[...].astype(F32) + jnp.sum(br_in[...].astype(F32), axis=0)).astype(BF16)
+        for p in range(nt):
+            added = jnp.sum(br_in[:, :, p * piece:(p + 1) * piece].astype(F32), axis=0)
+            own[p] = (own[p].astype(F32) + added).astype(BF16)
 
         wait_send(low_sum[0])
         wait_send(low_all[0])
-        wait_send(hid_sum[0])
+        for i in range(2):
+            pairs[i].wait_send()
+            wait_send(values[i][0])
         wait_send(hid_all[0])
         wait_send(down_sum[0])
         finish_down()
@@ -254,7 +298,8 @@
     lax.fori_loop(0, layers, layer, 0)
     wait_send(gain_send)
     wait_send(mask_sends)
-    out[...] = own[...]
+    for p in range(nt):
+        out[:, p * piece:(p + 1) * piece] = own[p]
 
 
 def body(
@@ -267,6 +312,7 @@
     fan = nt // ns
     span = rows * ns
     slab = span // nt
+    piece, chips = f_block // nt, nt // 2
     slots = max(nt, ns, ns * fan)
     weights = (gate_left, up_left, gate_right, up_right, down_left, down_right)
     vmem, hbm = pl.BlockSpec(memory_space=pltpu.VMEM), pl.BlockSpec(memory_space=pl.ANY)
@@ -280,22 +326,24 @@
             pltpu.VMEM((ns, fan, 1, f_block), F32),
             pltpu.VMEM((3, 1, rank), F32),
             pltpu.VMEM((ns, 3, 1, rank), F32),
-            pltpu.VMEM((rows, f_block), BF16),
-            pltpu.VMEM((ns, fan, rows, f_block), BF16),
-            pltpu.VMEM((ns, 3, rows, rank), F32),
-            pltpu.VMEM((ns, 3, rows, rank), F32),
+            pltpu.VMEM((nt, rows, piece), BF16),
+            pltpu.VMEM((nt, ns, fan, rows, piece), BF16),
+            pltpu.VMEM((ns, 3, rows, rank), BF16),
+            pltpu.VMEM((ns, 3, rows, rank), BF16),
             pltpu.VMEM((ns, 2, rows, rank), BF16),
-            pltpu.VMEM((nt, 2, slab, width), BF16),
-            pltpu.VMEM((nt, 2, slab, width), BF16),
+            pltpu.VMEM((2, 2, chips, slab, width), BF16),
+            pltpu.VMEM((2, chips, slab, width), BF16),
+            pltpu.VMEM((2, chips, slab, width), BF16),
+            pltpu.VMEM((2, chips, slab, width), BF16),
             pltpu.VMEM((nt, slab, width), BF16),
-            pltpu.VMEM((ns, rows, rank), F32),
-            pltpu.VMEM((ns, rows, rank), F32),
+            pltpu.VMEM((ns, rows, rank), BF16),
+            pltpu.VMEM((ns, rows, rank), BF16),
             pltpu.VMEM((rows, rank), BF16),
             pltpu.VMEM((ns, fan, rows, rank), BF16),
             pltpu.VMEM((ns, rows, f_block), BF16),
             pltpu.VMEM((ns, rows, f_block), BF16),
-            pltpu.SemaphoreType.DMA((9, slots)),
-            pltpu.SemaphoreType.DMA((9, slots)),
+            pltpu.SemaphoreType.DMA((PHASES, slots)),
+            pltpu.SemaphoreType.DMA((PHASES, slots)),
             pltpu.SemaphoreType.DMA((1, slots)),
             pltpu.SemaphoreType.DMA((1, slots)),
             pltpu.SemaphoreType.DMA((6, layers)),

time: 215 us -> 195 us (0.907)
  Pallas kernels: 212 us -> 191 us
    pallas_call x1, Pallas kernels: 212 us -> 191 us  [body(): pl.pallas_call(functools.partial(kernel, nt, ns, float(norm_gain.shape[1]...]
where the time goes in v2:
time: 195 us; the launch traced here: 194 us
  Pallas kernels  191 us (98%)
  local copies, waits for them, and re-layouts  2.88 us (1%)
    pallas_call x1, Pallas kernels, body(): pl.pallas_call(functools.partial(kernel, nt, ns, float(norm_gain.shape[1]...  191 us

profile of v2, /device:TPU:0, one launch (start us, length us, event | category | flops | bytes accessed | tf_op | source)
XLA Modules:
  0.0 194.3 jit_solution(7768108571967617427)
XLA Ops:
  0.0 0.0 copy-start
  0.0 0.8 copy-done
  0.8 0.0 copy-start.1
  0.8 0.8 copy-done.1
  1.6 0.0 copy-start.2
  1.6 0.7 copy-done.2
  2.3 191.4 %shard_map.91 = bf16[16,2048]{1,0:T(8,128)(2,1)S(1)} custom-call(bf16[16,2048]{1,0:T(8,128)(2,1)S(1)} %copy-done, f32[1,8192]{1,0:T(1,128)S(1)} %copy-done.1, s32[1,3]{1,0:T(1,128)S(1)} %copy-done.2, bf16[4,128,2048]{2,1,0:T(8,128)(2,1)} %gl_hbm.1, bf16[4,128,2048]{2,1,0:T(8,128)(2,1)} %ul_hbm.1, bf16[4,128,3584]{2,1,0:T(8,128)(2,1)} %gr_hbm.1, ...), custom_call_target="tpu_custom_call" | custom-call | flops 1107296256 | bytes 17301504 | tf_op jit(solution)/shard_map/pallas_call | solution.py:319
  193.6 0.6 copy.11
Async XLA Ops:
  0.0 0.8 copy-start
  0.8 0.8 copy-start.1
  1.6 0.7 copy-start.2

commit v3 on v2

--- a/solution.py
+++ b/solution.py
@@ -8,8 +8,8 @@
 from jax.sharding import PartitionSpec as P
 
 BF16, F32 = jnp.bfloat16, jnp.float32
-AUX, SPREAD, GATHER, GATE_SUM, GATE_ALL, PAIR, GATE_VALUES, UP_VALUES = range(8)
-HID_ALL, DOWN_SUM, DOWN_ALL, OUT_SUM, PHASES = range(8, 13)
+AUX, SPREAD, GATHER, GATE_SUM, SQUARES, PAIR, GATE_VALUES, UP_VALUES = range(8)
+HID_ALL, DOWN, OUT_SUM, PHASES = range(8, 12)
 
 
 def contract_last(left_side, right_side):
@@ -24,7 +24,7 @@
     out,
     gl, ul, gr, ur, dl, dr,
     gain_out, gain, mask_out, mask,
-    own, wide, low_out, low_in, low, val_out, pair_in, val_mid, val_in, hid, down_out, down_in,
+    own, wide, low_out, low_in, sq_out, sq_in, val_out, pair_in, val_mid, val_in, hid,
     dlow_own, dlow, br_out, br_in,
     send, recv, mask_send, mask_recv, load,
 ):
@@ -175,13 +175,12 @@
     )
     aux_first = spread(SPREAD, lambda j: own.at[j], lambda j: wide.at[j])
     gather = over_tensor(GATHER, lambda j: wide.at[t], lambda j: wide.at[j])
-    low_sum = over_section(GATE_SUM, lambda j: low_out.at[j], lambda j: low_in.at[j])
-    low_all = over_section(GATE_ALL, lambda j: low.at[s], lambda j: low.at[j])
+    low_sum = over_section(GATE_SUM, lambda j: low_out, lambda j: low_in.at[j])
+    sq_sum = over_section(SQUARES, lambda j: sq_out, lambda j: sq_in.at[j])
     pairs = [pair_copies(i) for i in range(2)]
     values = [over_chips(GATE_VALUES, 0), over_chips(UP_VALUES, 1)]
     hid_all = over_tensor(HID_ALL, lambda j: hid.at[t], lambda j: hid.at[j])
-    down_sum = over_section(DOWN_SUM, lambda j: down_out.at[j], lambda j: down_in.at[j])
-    down_all = spread(DOWN_ALL, lambda j: dlow_own, lambda j: dlow)
+    down_all = spread(DOWN, lambda j: dlow_own, lambda j: dlow)
     out_sum = over_section(OUT_SUM, lambda j: br_out.at[j], lambda j: br_in.at[j])
 
     start(gain_send)
@@ -217,24 +216,28 @@
                 scaled = (values_here * gains).astype(BF16)
                 gate_part += contract_last(scaled, gl[l, :, at:at + piece])
                 up_part += contract_last(scaled, ul[l, :, at:at + piece])
-        low_out[:, 0] = gate_part.astype(BF16).reshape(ns, rows, rank)
-        low_out[:, 1] = up_part.astype(BF16).reshape(ns, rows, rank)
-        low_out[:, 2] = jnp.broadcast_to(squares, (span, rank)).astype(BF16).reshape(ns, rows, rank)
+        low_out[0] = gate_part.astype(BF16)
+        low_out[1] = up_part.astype(BF16)
+        diagonal = lax.broadcasted_iota(jnp.int32, (span, span), 0) == lax.broadcasted_iota(
+            jnp.int32, (span, span), 1
+        )
+        sq_out[...] = jnp.sum(jnp.where(diagonal, squares, 0.0), axis=0, keepdims=True)
+        start(sq_sum[0])
         start(low_sum[0])
-        low_in[s] = low_out[s]
+        low_in[s] = low_out[...]
+        sq_in[s] = sq_out[...]
+        wait_recv(sq_sum[1])
+        square_row = jnp.sum(sq_in[...], axis=0)
+        square = jnp.sum(jnp.where(diagonal, square_row, 0.0), axis=1, keepdims=True)
+        scale = lax.rsqrt(square / features + 1e-05)
+        weights[2].wait()
+        weights[3].wait()
         wait_recv(low_sum[1])
         total = jnp.sum(low_in[...].astype(F32), axis=0)
-        scale = lax.rsqrt(total[2] / features + 1e-05)
-        low[s, 0] = (total[0] * scale * mask[l, 0]).astype(BF16)
-        low[s, 1] = (total[1] * scale * mask[l, 1]).astype(BF16)
-        start(low_all[0])
-        weights[2].wait()
-        weights[3].wait()
-        wait_recv(low_all[1])
+        gate_low = (total[0] * scale * mask[l, 0]).astype(BF16)
+        up_low = (total[1] * scale * mask[l, 1]).astype(BF16)
 
         width = gr.shape[2]
-        gate_low = low[:, 0].reshape(span, rank)
-        up_low = low[:, 1].reshape(span, rank)
         wait_send(gather[0])
         for i, (narrow, right) in enumerate(((gate_low, gr), (up_low, ur))):
             product = jnp.dot(narrow, right[l], preferred_element_type=F32).astype(BF16)
@@ -259,13 +262,8 @@
         weights[4].wait()
         wait_recv(hid_all[1])
 
-        down_out[...] = contract_last(
-            hid[...].reshape(span, width), dl[l]
-        ).astype(BF16).reshape(ns, rows, rank)
-        start(down_sum[0])
-        down_in[s] = down_out[s]
-        wait_recv(down_sum[1])
-        dlow_own[...] = (jnp.sum(down_in[...].astype(F32), axis=0) * mask[l, 2]).astype(BF16)
+        down_part = contract_last(hid[...].reshape(span, width), dl[l])
+        dlow_own[...] = (down_part * mask[l, 2]).astype(BF16)
         begin_down, arrive_down, finish_down = down_all
         begin_down()
         weights[5].wait()
@@ -274,7 +272,9 @@
         branch = jnp.zeros((span, f_block), F32)
         for kk in range(fan):
             at = kk * rank
-            branch += contract_last(dlow[:, kk].reshape(span, rank), dr[l, :, at:at + rank])
+            branch += contract_last(
+                jnp.sum(dlow[:, kk].astype(F32), axis=0).astype(BF16), dr[l, :, at:at + rank]
+            )
         br_out[...] = branch.astype(BF16).reshape(ns, rows, f_block)
         start(out_sum[0])
         br_in[s] = br_out[s]
@@ -285,12 +285,11 @@
             own[p] = (own[p].astype(F32) + added).astype(BF16)
 
         wait_send(low_sum[0])
-        wait_send(low_all[0])
+        wait_send(sq_sum[0])
         for i in range(2):
             pairs[i].wait_send()
             wait_send(values[i][0])
         wait_send(hid_all[0])
-        wait_send(down_sum[0])
         finish_down()
         wait_send(out_sum[0])
         return carry
@@ -328,18 +327,17 @@
             pltpu.VMEM((ns, 3, 1, rank), F32),
             pltpu.VMEM((nt, rows, piece), BF16),
             pltpu.VMEM((nt, ns, fan, rows, piece), BF16),
-            pltpu.VMEM((ns, 3, rows, rank), BF16),
-            pltpu.VMEM((ns, 3, rows, rank), BF16),
-            pltpu.VMEM((ns, 2, rows, rank), BF16),
+            pltpu.VMEM((2, span, rank), BF16),
+            pltpu.VMEM((ns, 2, span, rank), BF16),
+            pltpu.VMEM((1, span), F32),
+            pltpu.VMEM((ns, 1, span), F32),
             pltpu.VMEM((2, 2, chips, slab, width), BF16),
             pltpu.VMEM((2, chips, slab, width), BF16),
             pltpu.VMEM((2, chips, slab, width), BF16),
             pltpu.VMEM((2, chips, slab, width), BF16),
             pltpu.VMEM((nt, slab, width), BF16),
-            pltpu.VMEM((ns, rows, rank), BF16),
-            pltpu.VMEM((ns, rows, rank), BF16),
-            pltpu.VMEM((rows, rank), BF16),
-            pltpu.VMEM((ns, fan, rows, rank), BF16),
+            pltpu.VMEM((span, rank), BF16),
+            pltpu.VMEM((ns, fan, span, rank), BF16),
             pltpu.VMEM((ns, rows, f_block), BF16),
             pltpu.VMEM((ns, rows, f_block), BF16),
             pltpu.SemaphoreType.DMA((PHASES, slots)),

time: 195 us -> 178 us (0.913)
  Pallas kernels: 191 us -> 175 us
    pallas_call x1, Pallas kernels: 191 us -> 175 us  [body(): pl.pallas_call(functools.partial(kernel, nt, ns, float(norm_gain.shape[1]...]
where the time goes in v3:
time: 178 us
  Pallas kernels  175 us (98%)
  local copies, waits for them, and re-layouts  2.88 us (2%)
    pallas_call x1, Pallas kernels, body(): pl.pallas_call(functools.partial(kernel, nt, ns, float(norm_gain.shape[1]...  175 us

profile of v3, /device:TPU:0, one launch (start us, length us, event | category | flops | bytes accessed | tf_op | source)
XLA Modules:
  0.0 177.6 jit_solution(12936127783427582795)
XLA Ops:
  0.0 0.0 copy-start
  0.0 0.8 copy-done
  0.8 0.0 copy-start.1
  0.8 0.8 copy-done.1
  1.6 0.0 copy-start.2
  1.6 0.7 copy-done.2
  2.3 174.7 %shard_map.91 = bf16[16,2048]{1,0:T(8,128)(2,1)S(1)} custom-call(bf16[16,2048]{1,0:T(8,128)(2,1)S(1)} %copy-done, f32[1,8192]{1,0:T(1,128)S(1)} %copy-done.1, s32[1,3]{1,0:T(1,128)S(1)} %copy-done.2, bf16[4,128,2048]{2,1,0:T(8,128)(2,1)} %gl_hbm.1, bf16[4,128,2048]{2,1,0:T(8,128)(2,1)} %ul_hbm.1, bf16[4,128,3584]{2,1,0:T(8,128)(2,1)} %gr_hbm.1, ...), custom_call_target="tpu_custom_call" | custom-call | flops 1107296256 | bytes 17301504 | tf_op jit(solution)/shard_map/pallas_call | solution.py:318
  176.9 0.6 copy.11
Async XLA Ops:
  0.0 0.8 copy-start
  0.8 0.8 copy-start.1
  1.6 0.7 copy-start.2

commit v4 on v3

--- a/solution.py
+++ b/solution.py
@@ -9,7 +9,7 @@
 
 BF16, F32 = jnp.bfloat16, jnp.float32
 AUX, SPREAD, GATHER, GATE_SUM, SQUARES, PAIR, GATE_VALUES, UP_VALUES = range(8)
-HID_ALL, DOWN, OUT_SUM, PHASES = range(8, 12)
+HID_ALL, RELAY, DOWN, OUT_SUM, PHASES = range(8, 13)
 
 
 def contract_last(left_side, right_side):
@@ -179,7 +179,17 @@
     sq_sum = over_section(SQUARES, lambda j: sq_out, lambda j: sq_in.at[j])
     pairs = [pair_copies(i) for i in range(2)]
     values = [over_chips(GATE_VALUES, 0), over_chips(UP_VALUES, 1)]
-    hid_all = over_tensor(HID_ALL, lambda j: hid.at[t], lambda j: hid.at[j])
+    mine, theirs = hid.at[t], hid.at[sibling]
+    others = [lax.rem(chip + j, chips) for j in range(1, chips)]
+    hid_far = [copy_to(HID_ALL, mine, mine, p * 2 + core, t, p * 2 + core, s) for p in others]
+    hid_near = copy_to(HID_ALL, mine, mine, sibling, t, sibling, s)
+    far_in, relays, relays_in = [], [], []
+    for p in others:
+        got, due = p * 2 + core, p * 2 + 1 - core
+        far_in.append(copy_to(HID_ALL, mine, hid.at[got], got, got, got, s))
+        relays.append(copy_to(RELAY, hid.at[got], hid.at[got], p, p, sibling, s))
+        relays_in.append(copy_to(RELAY, hid.at[due], hid.at[due], p, p, sibling, s))
+    near_in = copy_to(HID_ALL, mine, theirs, sibling, sibling, sibling, s)
     down_all = spread(DOWN, lambda j: dlow_own, lambda j: dlow)
     out_sum = over_section(OUT_SUM, lambda j: br_out.at[j], lambda j: br_in.at[j])
 
@@ -258,13 +268,19 @@
             sums.append(jnp.sum(val_in[i].astype(F32), axis=0))
         gate_sum, up_sum = sums
         hid[t] = (gate_sum / (1.0 + jnp.exp(-gate_sum)) * up_sum).astype(BF16)
-        start(hid_all[0])
+        start(hid_far)
+        hid_near.start()
         weights[4].wait()
-        wait_recv(hid_all[1])
+        for arrived, relay in zip(far_in, relays):
+            arrived.wait_recv()
+            relay.start()
+        near_in.wait_recv()
+        wait_recv(relays_in)
 
         down_part = contract_last(hid[...].reshape(span, width), dl[l])
         dlow_own[...] = (down_part * mask[l, 2]).astype(BF16)
         begin_down, arrive_down, finish_down = down_all
+        wait_send(relays)
         begin_down()
         weights[5].wait()
         arrive_down()
@@ -289,7 +305,8 @@
         for i in range(2):
             pairs[i].wait_send()
             wait_send(values[i][0])
-        wait_send(hid_all[0])
+        wait_send(hid_far)
+        hid_near.wait_send()
         finish_down()
         wait_send(out_sum[0])
         return carry

time: 178 us -> 176 us (0.989)
  Pallas kernels: 175 us -> 173 us
    pallas_call x1, Pallas kernels: 175 us -> 173 us  [body(): pl.pallas_call(functools.partial(kernel, nt, ns, float(norm_gain.shape[1]...]
where the time goes in v4:
time: 176 us; the launch traced here: 175 us
  Pallas kernels  173 us (98%)
  local copies, waits for them, and re-layouts  2.88 us (2%)
    pallas_call x1, Pallas kernels, body(): pl.pallas_call(functools.partial(kernel, nt, ns, float(norm_gain.shape[1]...  173 us

profile of v4, /device:TPU:0, one launch (start us, length us, event | category | flops | bytes accessed | tf_op | source)
XLA Modules:
  0.0 175.5 jit_solution(10647466403365219851)
XLA Ops:
  0.0 0.0 copy-start
  0.0 0.8 copy-done
  0.8 0.0 copy-start.1
  0.8 0.8 copy-done.1
  1.6 0.0 copy-start.2
  1.6 0.7 copy-done.2
  2.3 172.6 %shard_map.91 = bf16[16,2048]{1,0:T(8,128)(2,1)S(1)} custom-call(bf16[16,2048]{1,0:T(8,128)(2,1)S(1)} %copy-done, f32[1,8192]{1,0:T(1,128)S(1)} %copy-done.1, s32[1,3]{1,0:T(1,128)S(1)} %copy-done.2, bf16[4,128,2048]{2,1,0:T(8,128)(2,1)} %gl_hbm.1, bf16[4,128,2048]{2,1,0:T(8,128)(2,1)} %ul_hbm.1, bf16[4,128,3584]{2,1,0:T(8,128)(2,1)} %gr_hbm.1, ...), custom_call_target="tpu_custom_call" | custom-call | flops 1107296256 | bytes 17301504 | tf_op jit(solution)/shard_map/pallas_call | solution.py:335
  174.8 0.6 copy.11
Async XLA Ops:
  0.0 0.8 copy-start
  0.8 0.8 copy-start.1
  1.6 0.7 copy-start.2
